TPU v7x, 32 devices: a whole 2x2x4 slice. The times are simulated.
32 devices in a mesh: rep: 16 (over z, x, core), fsdp: 2 (over y).
Axes of the slice: x: 2, y: 2, z: 4, core: 2. Of those that a mesh axis runs over, the one named last changes fastest.
Arguments:
- activations: float32 [16384, 960], P(('rep', 'fsdp')), may hold values from -6 to 6
- segments: int32 [16384], P(('rep', 'fsdp')), may hold values from 0 to 47, as said below
- q_weight: bfloat16 [960, 960], P('fsdp'), may hold values from -0.1875 to 0.1875
- k_weight: bfloat16 [960, 320], P('fsdp'), may hold values from -0.1875 to 0.1875
- v_weight: bfloat16 [960, 320], P('fsdp'), may hold values from -0.1875 to 0.1875
- o_weight: bfloat16 [960, 960], P('fsdp'), may hold values from -0.75 to 0.75
- gate_weight: bfloat16 [960, 2560], P('fsdp'), may hold values from -0.1875 to 0.1875
- up_weight: bfloat16 [960, 2560], P('fsdp'), may hold values from -0.1875 to 0.1875
- down_weight: bfloat16 [2560, 960], P('fsdp'), may hold values from -0.125 to 0.125
- attn_gain: bfloat16 [960], P('fsdp'), may hold values from 0.25 to 1.75
- ffn_gain: bfloat16 [960], P('fsdp'), may hold values from 0.25 to 1.75
- out_grad: float32 [16384, 960], P(('rep', 'fsdp')), may hold values from -6 to 6
Outputs:
- output: float32 [16384, 960], P(('rep', 'fsdp'))
- grad_activations: float32 [16384, 960], P(('rep', 'fsdp'))
- grad_q_weight: float32 [960, 960], P('fsdp')
- grad_k_weight: float32 [960, 320], P('fsdp')
- grad_v_weight: float32 [960, 320], P('fsdp')
- grad_o_weight: float32 [960, 960], P('fsdp')
- grad_gate_weight: float32 [960, 2560], P('fsdp')
- grad_up_weight: float32 [960, 2560], P('fsdp')
- grad_down_weight: float32 [2560, 960], P('fsdp')
- grad_attn_gain: float32 [960], P('fsdp')
- grad_ffn_gain: float32 [960], P('fsdp')
Inputs may be any that keep to these rules, and one draw needn't show every extreme that they name: `segments`: segment numbers never fall. Sequence s holds documents 3 s, 3 s + 1 and 3 s + 2 in that order; document 3 s + 1 starts within the first 512 tokens of the sequence and ends within its last 512.
All inputs are finite; a program needn't handle non-finite values.
Results may differ from a plain program's by a relative error of at most 0.023.
Values may be sent and summed in bfloat16 or wider, within the bound.
A program may use at most 192 MiB of HBM per device.

v0:
```python
import jax
import jax.numpy as jnp
from jax import lax
from jax.sharding import PartitionSpec as P

QH = 15
KVH = 5
HD = 64
KEYBLK = 512


epsilon = 1e-05
rope_base = 100000.0
masked_value = -1e30


def rotary_tables(positions):
    exponent = jnp.arange(HD // 2, dtype=jnp.float32) * 2.0 / HD
    inverse = rope_base ** (-exponent)
    angles = positions.astype(jnp.float32)[:, None] * inverse[None, :]
    angles = jnp.concatenate([angles, angles], axis=1)
    return (jnp.cos(angles), jnp.sin(angles))


def rotate(head_values, cosine_table, sine_table):
    half_width = head_values.shape[-1] // 2
    turned = jnp.concatenate(
        [-head_values[..., half_width:], head_values[..., :half_width]], axis=-1
    )
    return head_values * cosine_table[:, None, :] + turned * sine_table[:, None, :]


def rotate_back(head_grads, cosine_table, sine_table):
    half_width = head_grads.shape[-1] // 2
    spun = head_grads * sine_table[:, None, :]
    return head_grads * cosine_table[:, None, :] + jnp.concatenate(
        [spun[..., half_width:], -spun[..., :half_width]], axis=-1
    )


def rms_scale(values):
    return lax.rsqrt(jnp.mean(values * values, axis=-1, keepdims=True) + epsilon)


def norm_back(inputs, row_scale, gain_full, d_normed):
    weighted = d_normed * gain_full
    gain_term = jnp.sum(d_normed * inputs * row_scale, axis=0)
    d_inputs = row_scale * weighted - inputs * row_scale**3 * jnp.mean(
        weighted * inputs, axis=-1, keepdims=True
    )
    return (d_inputs, gain_term)


def body(
    activations,
    segments,
    q_weight,
    k_weight,
    v_weight,
    o_weight,
    gate_weight,
    up_weight,
    down_weight,
    attn_gain,
    ffn_gain,
    out_grad,
):
    rows_here = activations.shape[0]
    my_index = lax.axis_index("fsdp")
    length = rows_here * lax.axis_size("fsdp")
    groups = QH // KVH
    softmax_scale = HD ** (-0.5)
    block_count = length // KEYBLK
    gathered = (
        lax.all_gather(q_weight, "fsdp", axis=0, tiled=True),
        lax.all_gather(k_weight, "fsdp", axis=0, tiled=True),
        lax.all_gather(v_weight, "fsdp", axis=0, tiled=True),
        lax.all_gather(o_weight, "fsdp", axis=0, tiled=True),
        lax.all_gather(gate_weight, "fsdp", axis=0, tiled=True),
        lax.all_gather(up_weight, "fsdp", axis=0, tiled=True),
        lax.all_gather(down_weight, "fsdp", axis=0, tiled=True),
        lax.all_gather(attn_gain, "fsdp", axis=0, tiled=True),
        lax.all_gather(ffn_gain, "fsdp", axis=0, tiled=True),
    )
    full_q, full_k, full_v, full_o, full_gate, full_up, full_down, gain_attn, gain_ffn = gathered
    positions = my_index * rows_here + jnp.arange(rows_here, dtype=jnp.int32)
    last_position = my_index * rows_here + rows_here - 1
    cosine_table, sine_table = rotary_tables(positions)
    scale_one = rms_scale(activations)
    normed_one = (activations * scale_one * gain_attn.astype(jnp.float32)).astype(jnp.bfloat16)
    q_pre = jnp.dot(normed_one, full_q, preferred_element_type=jnp.float32)
    k_pre = jnp.dot(normed_one, full_k, preferred_element_type=jnp.float32)
    v_pre = jnp.dot(normed_one, full_v, preferred_element_type=jnp.float32)
    queries = rotate(q_pre.reshape(rows_here, QH, HD), cosine_table, sine_table).astype(
        jnp.bfloat16
    )
    queries = queries.reshape(rows_here, KVH, groups, HD)
    keys_low = rotate(k_pre.reshape(rows_here, KVH, HD), cosine_table, sine_table).astype(
        jnp.bfloat16
    )
    keys_low = keys_low.reshape(rows_here, KVH * HD)
    values_low = v_pre.astype(jnp.bfloat16)
    all_keys, all_values, all_segments = (
        lax.all_gather(keys_low, "fsdp", axis=0, tiled=True),
        lax.all_gather(values_low, "fsdp", axis=0, tiled=True),
        lax.all_gather(segments, "fsdp", axis=0, tiled=True),
    )

    def block_scores(block_index, key_source, segment_source):
        key_start = block_index * KEYBLK
        key_block = lax.dynamic_slice_in_dim(key_source, key_start, KEYBLK, 0).reshape(
            KEYBLK, KVH, HD
        )
        segment_block = lax.dynamic_slice_in_dim(segment_source, key_start, KEYBLK, 0)
        scores = (
            jnp.einsum("tkgd,skd->kgts", queries, key_block, preferred_element_type=jnp.float32)
            * softmax_scale
        )
        key_positions = key_start + jnp.arange(KEYBLK, dtype=jnp.int32)
        allowed = (segments[:, None] == segment_block[None, :]) & (
            key_positions[None, :] <= positions[:, None]
        )
        return (scores, allowed, key_block)

    def value_rows_of(block_index, value_source):
        return lax.dynamic_slice_in_dim(value_source, block_index * KEYBLK, KEYBLK, 0).reshape(
            KEYBLK, KVH, HD
        )

    def sum_block(block_index, state_pair):

        def sum_visit(state_now):
            running_top, running_sum = state_now
            scores, allowed, key_block = block_scores(block_index, all_keys, all_segments)
            masked = jnp.where(allowed, scores, masked_value)
            new_top = jnp.maximum(running_top, jnp.max(masked, axis=-1))
            exponent = jnp.where(allowed, jnp.exp(masked - new_top[..., None]), 0.0)
            return (
                new_top,
                running_sum * jnp.exp(running_top - new_top) + jnp.sum(exponent, axis=-1),
            )

        return lax.cond(
            block_index * KEYBLK <= last_position,
            sum_visit,
            lambda unchanged: unchanged,
            state_pair,
        )

    start_top = jnp.full((KVH, groups, rows_here), masked_value, jnp.float32)
    start_sum = jnp.zeros((KVH, groups, rows_here), jnp.float32)
    final_top, final_sum = lax.fori_loop(0, block_count, sum_block, (start_top, start_sum))
    log_total = final_top + jnp.log(final_sum)

    def value_block(block_index, accumulated):

        def value_visit(accumulated_now):
            scores, allowed, key_block = block_scores(block_index, all_keys, all_segments)
            probs_full = jnp.where(allowed, jnp.exp(scores - log_total[..., None]), 0.0)
            value_rows = value_rows_of(block_index, all_values)
            return accumulated_now + jnp.einsum(
                "kgts,skd->tkgd",
                probs_full.astype(jnp.bfloat16),
                value_rows,
                preferred_element_type=jnp.float32,
            )

        return lax.cond(
            block_index * KEYBLK <= last_position,
            value_visit,
            lambda unchanged: unchanged,
            accumulated,
        )

    attended = lax.fori_loop(
        0, block_count, value_block, jnp.zeros((rows_here, KVH, groups, HD), jnp.float32)
    )
    attn_low = attended.reshape(rows_here, QH * HD).astype(jnp.bfloat16)
    middle = activations + jnp.dot(attn_low, full_o, preferred_element_type=jnp.float32)
    scale_two = rms_scale(middle)
    normed_two = (middle * scale_two * gain_ffn.astype(jnp.float32)).astype(jnp.bfloat16)
    gate_pre = jnp.dot(normed_two, full_gate, preferred_element_type=jnp.float32)
    up_pre = jnp.dot(normed_two, full_up, preferred_element_type=jnp.float32)
    sigmoid_gate = jax.nn.sigmoid(gate_pre)
    silu_gate = gate_pre * sigmoid_gate
    hidden_low = (silu_gate * up_pre).astype(jnp.bfloat16)
    result = middle + jnp.dot(hidden_low, full_down, preferred_element_type=jnp.float32)
    back_set = (
        lax.all_gather(q_weight, "fsdp", axis=0, tiled=True),
        lax.all_gather(k_weight, "fsdp", axis=0, tiled=True),
        lax.all_gather(v_weight, "fsdp", axis=0, tiled=True),
        lax.all_gather(o_weight, "fsdp", axis=0, tiled=True),
        lax.all_gather(gate_weight, "fsdp", axis=0, tiled=True),
        lax.all_gather(up_weight, "fsdp", axis=0, tiled=True),
        lax.all_gather(down_weight, "fsdp", axis=0, tiled=True),
        lax.all_gather(attn_gain, "fsdp", axis=0, tiled=True),
        lax.all_gather(ffn_gain, "fsdp", axis=0, tiled=True),
    )
    back_q, back_k, back_v, back_o, back_gate, back_up, back_down, back_gain_attn, back_gain_ffn = (
        back_set
    )
    key_source, value_source, segment_source = (all_keys, all_values, all_segments)
    cot_low = out_grad.astype(jnp.bfloat16)
    grad_down = jnp.einsum("tf,td->fd", hidden_low, cot_low, preferred_element_type=jnp.float32)
    d_hidden = jnp.einsum("td,fd->tf", cot_low, back_down, preferred_element_type=jnp.float32)
    d_gate = (d_hidden * up_pre * sigmoid_gate * (1.0 + gate_pre * (1.0 - sigmoid_gate))).astype(
        jnp.bfloat16
    )
    d_up = (d_hidden * silu_gate).astype(jnp.bfloat16)
    grad_gate = jnp.einsum("tc,tf->cf", normed_two, d_gate, preferred_element_type=jnp.float32)
    grad_up = jnp.einsum("tc,tf->cf", normed_two, d_up, preferred_element_type=jnp.float32)
    d_normed_two = jnp.einsum("tf,cf->tc", d_gate, back_gate, preferred_element_type=jnp.float32)
    d_normed_two = d_normed_two + jnp.einsum(
        "tf,cf->tc", d_up, back_up, preferred_element_type=jnp.float32
    )
    d_norm_ffn, grad_ffn_term = norm_back(
        middle, scale_two, back_gain_ffn.astype(jnp.float32), d_normed_two
    )
    d_middle = out_grad + d_norm_ffn
    d_branch = d_middle.astype(jnp.bfloat16)
    grad_o = jnp.einsum("tc,td->cd", attn_low, d_branch, preferred_element_type=jnp.float32)
    d_attended = jnp.einsum(
        "td,cd->tc", d_branch, back_o, preferred_element_type=jnp.float32
    ).astype(jnp.bfloat16)
    d_attended = d_attended.reshape(rows_here, KVH, groups, HD)
    row_delta = jnp.einsum("tkgd,tkgd->kgt", d_attended.astype(jnp.float32), attended)

    def grad_block(d_queries, block_index):

        def grad_visit(d_queries_now):
            scores, allowed, key_block = block_scores(block_index, key_source, segment_source)
            value_rows = value_rows_of(block_index, value_source)
            probs_full = jnp.where(allowed, jnp.exp(scores - log_total[..., None]), 0.0)
            d_values = jnp.einsum(
                "kgts,tkgd->skd",
                probs_full.astype(jnp.bfloat16),
                d_attended,
                preferred_element_type=jnp.float32,
            )
            d_probs = jnp.einsum(
                "tkgd,skd->kgts", d_attended, value_rows, preferred_element_type=jnp.float32
            )
            d_scores = (probs_full * (d_probs - row_delta[..., None])).astype(jnp.bfloat16)
            d_queries_now = (
                d_queries_now
                + jnp.einsum(
                    "kgts,skd->tkgd", d_scores, key_block, preferred_element_type=jnp.float32
                )
                * softmax_scale
            )
            d_keys = (
                jnp.einsum("kgts,tkgd->skd", d_scores, queries, preferred_element_type=jnp.float32)
                * softmax_scale
            )
            return (
                d_queries_now,
                (d_keys.reshape(KEYBLK, KVH * HD), d_values.reshape(KEYBLK, KVH * HD)),
            )

        def skip(d_queries_now):
            empty_rows = jnp.zeros((KEYBLK, KVH * HD), jnp.float32)
            return (d_queries_now, (empty_rows, empty_rows))

        return lax.cond(block_index * KEYBLK <= last_position, grad_visit, skip, d_queries)

    start_grads = jnp.zeros((rows_here, KVH, groups, HD), jnp.float32)
    d_queries, (key_terms, value_terms) = lax.scan(
        grad_block, start_grads, jnp.arange(block_count, dtype=jnp.int32)
    )
    key_terms = key_terms.reshape(length, KVH * HD)
    value_terms = value_terms.reshape(length, KVH * HD)
    d_keys_sum, d_values_sum = (
        lax.psum_scatter(
            key_terms.astype(jnp.bfloat16), "fsdp", scatter_dimension=0, tiled=True
        ).astype(jnp.float32),
        lax.psum_scatter(
            value_terms.astype(jnp.bfloat16), "fsdp", scatter_dimension=0, tiled=True
        ).astype(jnp.float32),
    )
    dq_low = (
        rotate_back(d_queries.reshape(rows_here, QH, HD), cosine_table, sine_table)
        .astype(jnp.bfloat16)
        .reshape(rows_here, QH * HD)
    )
    dk_low = (
        rotate_back(d_keys_sum.reshape(rows_here, KVH, HD), cosine_table, sine_table)
        .astype(jnp.bfloat16)
        .reshape(rows_here, KVH * HD)
    )
    dv_low = d_values_sum.astype(jnp.bfloat16)
    grad_q = jnp.einsum("tc,tq->cq", normed_one, dq_low, preferred_element_type=jnp.float32)
    grad_k = jnp.einsum("tc,tq->cq", normed_one, dk_low, preferred_element_type=jnp.float32)
    grad_v = jnp.einsum("tc,tq->cq", normed_one, dv_low, preferred_element_type=jnp.float32)
    d_normed_one = jnp.einsum("tq,cq->tc", dq_low, back_q, preferred_element_type=jnp.float32)
    d_normed_one = d_normed_one + jnp.einsum(
        "tq,cq->tc", dk_low, back_k, preferred_element_type=jnp.float32
    )
    d_normed_one = d_normed_one + jnp.einsum(
        "tq,cq->tc", dv_low, back_v, preferred_element_type=jnp.float32
    )
    d_norm_attn, grad_attn_term = norm_back(
        activations, scale_one, back_gain_attn.astype(jnp.float32), d_normed_one
    )
    grad_activations = d_middle + d_norm_attn
    shares = (
        lax.psum_scatter(
            grad_q.astype(jnp.bfloat16), "fsdp", scatter_dimension=0, tiled=True
        ).astype(jnp.float32),
        lax.psum_scatter(
            grad_k.astype(jnp.bfloat16), "fsdp", scatter_dimension=0, tiled=True
        ).astype(jnp.float32),
        lax.psum_scatter(
            grad_v.astype(jnp.bfloat16), "fsdp", scatter_dimension=0, tiled=True
        ).astype(jnp.float32),
        lax.psum_scatter(
            grad_o.astype(jnp.bfloat16), "fsdp", scatter_dimension=0, tiled=True
        ).astype(jnp.float32),
        lax.psum_scatter(
            grad_gate.astype(jnp.bfloat16), "fsdp", scatter_dimension=0, tiled=True
        ).astype(jnp.float32),
        lax.psum_scatter(
            grad_up.astype(jnp.bfloat16), "fsdp", scatter_dimension=0, tiled=True
        ).astype(jnp.float32),
        lax.psum_scatter(
            grad_down.astype(jnp.bfloat16), "fsdp", scatter_dimension=0, tiled=True
        ).astype(jnp.float32),
        lax.psum_scatter(
            grad_attn_term.astype(jnp.bfloat16), "fsdp", scatter_dimension=0, tiled=True
        ).astype(jnp.float32),
        lax.psum_scatter(
            grad_ffn_term.astype(jnp.bfloat16), "fsdp", scatter_dimension=0, tiled=True
        ).astype(jnp.float32),
    )
    totals = (
        lax.psum(shares[0].astype(jnp.bfloat16), "rep").astype(jnp.float32),
        lax.psum(shares[1].astype(jnp.bfloat16), "rep").astype(jnp.float32),
        lax.psum(shares[2].astype(jnp.bfloat16), "rep").astype(jnp.float32),
        lax.psum(shares[3].astype(jnp.bfloat16), "rep").astype(jnp.float32),
        lax.psum(shares[4].astype(jnp.bfloat16), "rep").astype(jnp.float32),
        lax.psum(shares[5].astype(jnp.bfloat16), "rep").astype(jnp.float32),
        lax.psum(shares[6].astype(jnp.bfloat16), "rep").astype(jnp.float32),
        lax.psum(shares[7].astype(jnp.bfloat16), "rep").astype(jnp.float32),
        lax.psum(shares[8].astype(jnp.bfloat16), "rep").astype(jnp.float32),
    )
    return (
        result,
        grad_activations,
        totals[0],
        totals[1],
        totals[2],
        totals[3],
        totals[4],
        totals[5],
        totals[6],
        totals[7],
        totals[8],
    )


def solution(mesh):
    placed = (
        P(("rep", "fsdp"), None),
        P(("rep", "fsdp")),
        P("fsdp", None),
        P("fsdp", None),
        P("fsdp", None),
        P("fsdp", None),
        P("fsdp", None),
        P("fsdp", None),
        P("fsdp", None),
        P("fsdp"),
        P("fsdp"),
        P(("rep", "fsdp"), None),
    )
    return jax.shard_map(
        body,
        mesh=mesh,
        in_specs=placed,
        out_specs=(
            P(("rep", "fsdp"), None),
            P(("rep", "fsdp"), None),
            P("fsdp", None),
            P("fsdp", None),
            P("fsdp", None),
            P("fsdp", None),
            P("fsdp", None),
            P("fsdp", None),
            P("fsdp", None),
            P("fsdp"),
            P("fsdp"),
        ),
        check_vma=False,
    )
```

profile of v0, /device:TPU:0, one launch (start us, length us, event | category | flops | bytes accessed | tf_op | source)
XLA Modules:
  0.0 946.1 jit_solution(4023045253003790022)
XLA Ops:
  10.7 12.7 %all-gather = bf16[2,480,320]{1,2,0:T(8,128)(2,1)S(1)} all-gather(bf16[1,480,320]{1,2,0:T(8,128)(2,1)S(1)} %bitcast.215), channel_id=1, replica_groups=mesh['rep'=16,'fsdp'=2] {'fsdp'}, dimensions={0}, use_global_device_ids=true | all-gather | bytes 921600 | tf_op jit(solution)/shard_map/all_gather | solution.py:77
  33.6 16.9 %all-gather.2 = bf16[2,480,320]{1,2,0:T(8,128)(2,1)S(1)} all-gather(bf16[1,480,320]{1,2,0:T(8,128)(2,1)S(1)} %bitcast.216), channel_id=1, replica_groups=mesh['rep'=16,'fsdp'=2] {'fsdp'}, dimensions={0}, use_global_device_ids=true | all-gather | bytes 921600 | tf_op jit(solution)/shard_map/all_gather | solution.py:76
  59.9 18.0 %all_gather.47 = bf16[1024,320]{0,1:T(8,128)(2,1)S(1)} all-gather(bf16[512,320]{0,1:T(8,128)(2,1)S(1)} %convolution_convert_fusion.8), channel_id=1, replica_groups=mesh['rep'=16,'fsdp'=2] {'fsdp'}, dimensions={0}, use_global_device_ids=true | all-gather | bytes 983040 | tf_op jit(solution)/shard_map/all_gather | solution.py:105
  77.9 14.7 %all_gather.50 = bf16[1024,320]{0,1:T(8,128)(2,1)S(1)} all-gather(bf16[512,320]{0,1:T(8,128)(2,1)S(1)} %fusion.30), channel_id=1, replica_groups=mesh['rep'=16,'fsdp'=2] {'fsdp'}, dimensions={0}, use_global_device_ids=true | all-gather | bytes 983040 | tf_op jit(solution)/shard_map/all_gather | solution.py:104
  96.3 19.0 %while.51 = (s32[]{:T(128)}, f32[5,3,512]{2,1,0:T(4,128)S(1)}, f32[5,3,512]{2,1,0:T(4,128)S(1)}, s32[]{:T(128)}, s32[512]{0:T(512)S(1)}, /*index=5*/s32[1024]{0:...) while((s32[]{:T(128)}, f32[5,3,512]{2,1,0:T(4,128)S(1)}, ...), condition=%wide.region_6.7_spmd.clone, body=%wide.region_1.6_spmd.clone.sunk | while | flops 535576576 | bytes 34629952 | solution.py:152
  96.8 18.4 %conditional.9 = ((f32[5,3,512]{2,1,0:T(4,128)S(1)}, f32[5,3,512]{2,1,0:T(4,128)S(1)})) conditional(s32[]{:T(128)} %convert_element_type.267, (f32[5,3,512]{2,1,0:T(4,128)S(1)}, f32[5,3,512]{2,1,0:T(4,128)S(1)}) %tuple.137, (s32[512]{0:T(512)S(1)}, s32[]{:T(128)}, s32[1024]{0:T(1024)S(1)}, s32[]{:T(128)}, bf16[1024,320]{0,1:T(8,128)(2,1)S(1)}, ...), branch_computations={%region_2.0_spmd, %region_3.5_spmd} | conditional | flops 535576576 | bytes 34627672 | solution.py:143
  104.3 10.9 %select_reduce_fusion = f32[5,3,512]{2,1,0:T(4,128)S(1)} fusion(f32[5,512,512,3]{2,1,3,0:T(8,128)} %get-tuple-element.725, f32[5,3,512]{2,1,0:T(4,128)S(1)} %max.2, pred[512,512]{0,1:T(8,128)(4,1)S(1)} %compare_and_fusion), kind=kLoop, calls=%fused_computation.4 | loop fusion | flops 19653120 | bytes 16052224 | tf_op jit(solution)/shard_map/while/body/eval_jaxpr/cond/branch_1_fun/reduce_sum | solution.py:140
  132.1 30.1 %all-gather.13.cloned.1.call-done = bf16[960,2560]{1,0:T(8,128)(2,1)} async-done(((bf16[480,2560]{1,0:T(8,128)(2,1)}), bf16[960,2560]{1,0:T(8,128)(2,1)}) %all-gather.13.cloned.1.call-update) | async-done | bytes 4915216 | tf_op jit(solution)/shard_map/all_gather | solution.py:79
  169.4 59.1 %all-gather.15.cloned.1.call-done = bf16[960,2560]{1,0:T(8,128)(2,1)} async-done(((bf16[480,2560]{1,0:T(8,128)(2,1)}), bf16[960,2560]{1,0:T(8,128)(2,1)}) %all-gather.15.cloned.1.call-update) | async-done | bytes 4915216 | tf_op jit(solution)/shard_map/all_gather | solution.py:80
  235.6 59.2 %all-gather.17.cloned.1.call-done = bf16[2560,960]{0,1:T(8,128)(2,1)} async-done(((bf16[1280,960]{0,1:T(8,128)(2,1)}), bf16[2560,960]{0,1:T(8,128)(2,1)}) %all-gather.17.cloned.1.call-update) | async-done | bytes 4915216 | tf_op jit(solution)/shard_map/all_gather | solution.py:81
  294.8 10.7 %multiply_convert_fusion = (bf16[512,2560]{1,0:T(8,128)(2,1)S(1)}, bf16[512,2560]{1,0:T(8,128)(2,1)S(1)}, bf16[512,2560]{1,0:T(8,128)(2,1)}) fusion(f32[512,2560]{1,0:T(8,128)} %fusion.45, f32[512,2560]{1,0:T(8,128)} %fusion.46, bf16[2560,960]{0,1:T(8,128)(2,1)} %all-gather.17.cloned.1.call-done, f32[512,960]{0,1:T(8,128)} %param.35), kind=kOutput, calls=%fused_computation.48 | convolution fusion | flops 2536734720 | bytes 25231360 | tf_op jit(solution)/shard_map/td,fd->tf/dot_general | solution.py:205
  320.2 37.2 %while.53 = (s32[]{:T(128)}, f32[512,5,3,64]{0,3,2,1:T(8,128)S(1)}, bf16[2,512,320]{1,2,0:T(8,128)(2,1)}, bf16[2,512,320]{1,2,0:T(8,128)(2,1)}, s32[2]{0:T(128)S...) while((s32[]{:T(128)}, f32[512,5,3,64]{0,3,2,1:T(8,128)S(1)}, ...), condition=%wide.region_16.17_spmd.clone, body=%wide.region_13.16_spmd.clone.sunk | while | flops 2558002176 | bytes 87734688 | solution.py:267
  321.7 29.9 %conditional.11 = (f32[512,5,3,64]{0,3,2,1:T(8,128)S(1)}, bf16[1,512,320]{1,2,0:T(8,128)(2,1)S(1)}, bf16[1,512,320]{1,2,0:T(8,128)(2,1)}) conditional(s32[]{:T(128)} %convert_element_type.269, f32[512,5,3,64]{0,3,2,1:T(8,128)S(1)} %get-tuple-element.1079, (s32[]{:T(128)}, bf16[1024,320]{0,1:T(8,128)(2,1)}, s32[512]{0:T(512)S(1)}, ...), branch_computations={%region_14.14_spmd, %region_15.15_spmd} | conditional | flops 2558002176 | bytes 86421616 | solution.py:264
  331.6 8.3 fusion.14
  343.8 7.8 fusion.18
  360.7 44.2 %reduce-scatter.14.cloned.1.call-done = bf16[512,320]{0,1:T(8,128)(2,1)} async-done(((bf16[1024,320]{0,1:T(8,128)(2,1)}), bf16[512,320]{0,1:T(8,128)(2,1)}) %reduce-scatter.14.cloned.1.call-update) | async-done | bytes 327696 | tf_op jit(solution)/shard_map/reduce_scatter | solution.py:273
  411.0 12.8 %reduce-scatter.16.cloned.1.call-done = bf16[512,320]{0,1:T(8,128)(2,1)} async-done(((bf16[1024,320]{0,1:T(8,128)(2,1)}), bf16[512,320]{0,1:T(8,128)(2,1)}) %reduce-scatter.16.cloned.1.call-update) | async-done | bytes 327696 | tf_op jit(solution)/shard_map/reduce_scatter | solution.py:276
  464.1 31.2 %reduce-scatter.18.cloned.1.call-done = bf16[480,960]{1,0:T(8,128)(2,1)} async-done(((bf16[960,960]{1,0:T(8,128)(2,1)}), bf16[480,960]{1,0:T(8,128)(2,1)}) %reduce-scatter.18.cloned.1.call-update) | async-done | bytes 921616 | tf_op jit(solution)/shard_map/reduce_scatter | solution.py:306
  495.3 33.3 %reduce-scatter.20.cloned.1.call-done = bf16[480,960]{1,0:T(8,128)(2,1)} async-done(((bf16[960,960]{1,0:T(8,128)(2,1)}), bf16[480,960]{1,0:T(8,128)(2,1)}) %reduce-scatter.20.cloned.1.call-update) | async-done | bytes 921616 | tf_op jit(solution)/shard_map/reduce_scatter | solution.py:315
  528.6 64.9 %reduce-scatter.22.cloned.1.call-done = bf16[480,2560]{1,0:T(8,128)(2,1)} async-done(((bf16[960,2560]{1,0:T(8,128)(2,1)}), bf16[480,2560]{1,0:T(8,128)(2,1)}) %reduce-scatter.22.cloned.1.call-update) | async-done | bytes 2457616 | tf_op jit(solution)/shard_map/reduce_scatter | solution.py:318
  593.5 65.1 %reduce-scatter.24.cloned.1.call-done = bf16[480,2560]{1,0:T(8,128)(2,1)} async-done(((bf16[960,2560]{1,0:T(8,128)(2,1)}), bf16[480,2560]{1,0:T(8,128)(2,1)}) %reduce-scatter.24.cloned.1.call-update) | async-done | bytes 2457616 | tf_op jit(solution)/shard_map/reduce_scatter | solution.py:321
  658.6 64.9 %reduce-scatter.26.cloned.1.call-done = bf16[1280,960]{0,1:T(8,128)(2,1)} async-done(((bf16[2560,960]{0,1:T(8,128)(2,1)}), bf16[1280,960]{0,1:T(8,128)(2,1)}) %reduce-scatter.26.cloned.1.call-update) | async-done | bytes 2457616 | tf_op jit(solution)/shard_map/reduce_scatter | solution.py:324
  744.0 34.8 %all-reduce.4 = (bf16[480]{0:T(512)(128)(2,1)S(1)}, bf16[480]{0:T(512)(128)(2,1)S(1)}) all-reduce(bf16[480]{0:T(512)(128)(2,1)S(1)} %dynamic-slice.3, bf16[480]{0:T(512)(128)(2,1)S(1)} %dynamic-slice.5), channel_id=1, replica_groups=mesh['rep'=16,'fsdp'=2] {'rep'}, use_global_device_ids=true, to_apply=%region_36.37 | all-reduce | flops 960 | bytes 3840 | tf_op jit(solution)/shard_map/psum | solution.py:342
  783.8 140.8 %all-reduce.10.cloned.1.call-done = (bf16[480,960]{1,0:T(8,128)(2,1)}, bf16[480,320]{0,1:T(8,128)(2,1)}, bf16[480,320]{0,1:T(8,128)(2,1)}, bf16[480,960]{1,0:T(8...) async-done(((bf16[480,960]{1,0:T(8,128)(2,1)}, bf16[480,320]{0,1:T(8,128)(2,1)}, bf16[480,320]{0,1:T(8,128)(2,1)}, ...) | async-done | bytes 9830416 | tf_op jit(solution)/shard_map/psum | solution.py:335
  (272 shorter events, 202.5 us)
Async XLA Ops:
  7.2 85.4 %all-gather.9.cloned.1.call-start = ((), (), s32[]{:S(2)}) async-start(), calls=%async_computation.9 | async-start | bytes 2949120 | tf_op jit(solution)/shard_map/all_gather | solution.py:75
  7.9 118.9 %all-gather.11.cloned.1.call-start = ((), (), s32[]{:S(2)}) async-start(), calls=%async_computation.10 | async-start | bytes 2949120 | tf_op jit(solution)/shard_map/all_gather | solution.py:78
  8.7 153.5 %all-gather.13.cloned.1.call-start = ((), (), s32[]{:S(2)}) async-start(), calls=%async_computation.11 | async-start | bytes 7372800 | tf_op jit(solution)/shard_map/all_gather | solution.py:79
  9.4 219.1 %all-gather.15.cloned.1.call-start = ((), (), s32[]{:S(2)}) async-start(), calls=%async_computation.12 | async-start | bytes 7372800 | tf_op jit(solution)/shard_map/all_gather | solution.py:80
  10.0 284.8 %all-gather.17.cloned.1.call-start = ((), (), s32[]{:S(2)}) async-start(), calls=%async_computation.13 | async-start | bytes 7372800 | tf_op jit(solution)/shard_map/all_gather | solution.py:81
  10.6 22.2 %copy-start.1 = (f32[512,960]{0,1:T(8,128)S(1)}, f32[512,960]{0,1:T(8,128)}, u32[]{:S(2)}) copy-start(f32[512,960]{0,1:T(8,128)} %param.24) | copy-start | bytes 5898244
  10.6 394.3 %reduce-scatter.14.cloned.1.call-start = ((), (), s32[]{:S(2)}) async-start(), calls=%async_computation.14 | async-start | bytes 983040 | tf_op jit(solution)/shard_map/reduce_scatter | solution.py:273
  32.8 20.2 %copy-start.43 = (f32[960]{0:T(1024)}, f32[960]{0:T(1024)S(1)}, u32[]{:S(2)}) copy-start(f32[960]{0:T(1024)S(1)} %convert_element_type.180) | copy-start | bytes 11524
  52.9 42.8 %copy-start.17 = (f32[512,64]{0,1:T(8,128)}, f32[512,64]{0,1:T(8,128)S(1)}, u32[]{:S(2)}) copy-start(f32[512,64]{0,1:T(8,128)S(1)} %get-tuple-element.749) | copy-start | bytes 393220
  53.0 42.8 %copy-start.19 = (f32[512,64]{0,1:T(8,128)}, f32[512,64]{0,1:T(8,128)S(1)}, u32[]{:S(2)}) copy-start(f32[512,64]{0,1:T(8,128)S(1)} %get-tuple-element.750) | copy-start | bytes 393220
  53.7 38.9 %copy-start.5 = (bf16[512,960]{0,1:T(8,128)(2,1)}, bf16[512,960]{0,1:T(8,128)(2,1)S(1)}, u32[]{:S(2)}) copy-start(bf16[512,960]{0,1:T(8,128)(2,1)S(1)} %multiply_convert_fusion.4) | copy-start | bytes 2949124
  132.1 96.4 %copy-start.7 = (bf16[512,960]{0,1:T(8,128)(2,1)}, bf16[512,960]{0,1:T(8,128)(2,1)S(1)}, u32[]{:S(2)}) copy-start(bf16[512,960]{0,1:T(8,128)(2,1)S(1)} %multiply_convert_fusion.3) | copy-start | bytes 2949124
  357.5 47.4 %copy-start.20 = (f32[512,64]{0,1:T(8,128)S(1)}, f32[512,64]{0,1:T(8,128)}, u32[]{:S(2)}) copy-start(f32[512,64]{0,1:T(8,128)} %copy-done.19) | copy-start | bytes 393220
  359.6 64.2 %reduce-scatter.16.cloned.1.call-start = ((), (), s32[]{:S(2)}) async-start(), calls=%async_computation.15 | async-start | bytes 983040 | tf_op jit(solution)/shard_map/reduce_scatter | solution.py:276
  360.6 45.5 %copy-start.18 = (f32[512,64]{0,1:T(8,128)S(1)}, f32[512,64]{0,1:T(8,128)}, u32[]{:S(2)}) copy-start(f32[512,64]{0,1:T(8,128)} %copy-done.17) | copy-start | bytes 393220
  360.6 98.2 %reduce-scatter.28.cloned.1.call-start = ((), (), s32[]{:S(2)}) async-start(), calls=%async_computation.21 | async-start | bytes 1105920
  410.9 51.3 %reduce-scatter.30.cloned.1.call-start = ((), (), s32[]{:S(2)}) async-start(), calls=%async_computation.22 | async-start | bytes 1105920
  428.5 66.9 %reduce-scatter.18.cloned.1.call-start = ((), (), s32[]{:S(2)}) async-start(), calls=%async_computation.16 | async-start | bytes 2949120 | tf_op jit(solution)/shard_map/reduce_scatter | solution.py:306
  433.6 95.1 %reduce-scatter.20.cloned.1.call-start = ((), (), s32[]{:S(2)}) async-start(), calls=%async_computation.17 | async-start | bytes 2949120 | tf_op jit(solution)/shard_map/reduce_scatter | solution.py:315
  437.6 155.9 %reduce-scatter.22.cloned.1.call-start = ((), (), s32[]{:S(2)}) async-start(), calls=%async_computation.18 | async-start | bytes 7372800 | tf_op jit(solution)/shard_map/reduce_scatter | solution.py:318
  444.9 213.7 %reduce-scatter.24.cloned.1.call-start = ((), (), s32[]{:S(2)}) async-start(), calls=%async_computation.19 | async-start | bytes 7372800 | tf_op jit(solution)/shard_map/reduce_scatter | solution.py:321
  451.1 272.4 %reduce-scatter.26.cloned.1.call-start = ((), (), s32[]{:S(2)}) async-start(), calls=%async_computation.20 | async-start | bytes 7372800 | tf_op jit(solution)/shard_map/reduce_scatter | solution.py:324
  458.7 465.9 %all-reduce.10.cloned.1.call-start = ((), (), s32[]{:S(2)}) async-start(), calls=%async_computation.23 | async-start | bytes 19988480 | tf_op jit(solution)/shard_map/psum | solution.py:335
  736.5 43.4 %copy-start.47 = (f32[512]{0:T(512)S(1)}, f32[512]{0:T(512)}, u32[]{:S(2)}) copy-start(f32[512]{0:T(512)} %get-tuple-element.751) | copy-start | bytes 6148
  (48 other events, 215.7 us)
Sparse Core Ops, SparseCore 0:
  9.6 41.4 all-gather.8
  52.6 43.1 all-gather.10
  97.3 64.8 all-gather.12
  163.6 64.8 all-gather.14
  229.9 64.8 all-gather.16
  359.7 45.1 reduce-scatter.13
  407.8 15.9 reduce-scatter.15
  426.1 16.8 reduce-scatter.27
  445.3 16.8 reduce-scatter.29
  464.9 30.3 reduce-scatter.17
  498.2 30.3 reduce-scatter.19
  531.4 62.0 reduce-scatter.21
  596.4 62.1 reduce-scatter.23
  661.4 62.1 reduce-scatter.25
  728.1 196.4 all-reduce.9
where the time goes:
time: 953 us; the launch traced here: 946 us
  waiting for transfers between devices  611 us (64%)
  matrix products  124 us (13%)
  blocking collectives  112 us (12%)
  local copies, waits for them, and re-layouts  40 us (4%)
  other arithmetic  39.7 us (4%)
  between operations  16.6 us (2%)
    psum x1, waiting for transfers between devices, body(): lax.psum(shares[0].astype(jnp.bfloat16), 'rep').astype(jnp.float32)  141 us
    reduce_scatter x1, waiting for transfers between devices, body(): lax.psum_scatter(grad_up.astype(jnp.bfloat16), 'fsdp', scatter_dimension=...  65.1 us
    reduce_scatter x1, waiting for transfers between devices, body(): lax.psum_scatter(grad_down.astype(jnp.bfloat16), 'fsdp', scatter_dimensio...  64.9 us
    reduce_scatter x1, waiting for transfers between devices, body(): lax.psum_scatter(grad_gate.astype(jnp.bfloat16), 'fsdp', scatter_dimensio...  64.9 us
    all_gather x1, waiting for transfers between devices, body(): lax.all_gather(down_weight, 'fsdp', axis=0, tiled=True)  59.2 us
    all_gather x1, waiting for transfers between devices, body(): lax.all_gather(up_weight, 'fsdp', axis=0, tiled=True)  59.1 us
    reduce_scatter x1, waiting for transfers between devices, body(): lax.psum_scatter(key_terms.astype(jnp.bfloat16), 'fsdp', scatter_dimensio...  44.2 us
    psum x1, blocking collectives, body(): lax.psum(shares[7].astype(jnp.bfloat16), 'rep').astype(jnp.float32)  34.8 us
  transfers between devices with their start and end apart: 15, of which 12 were waited for; matrix products, arithmetic and copies ran while one was open for 12% of the time, Pallas kernels for 0%

commit v1 on v0

--- a/solution.py
+++ b/solution.py
@@ -49,6 +49,95 @@
         weighted * inputs, axis=-1, keepdims=True
     )
     return (d_inputs, gain_term)
+
+
+def axis_bits(axis):
+    size = lax.axis_size(axis)
+    bits = []
+    bit = 1
+    while bit < size:
+        bits.append(bit)
+        bit *= 2
+    return bits
+
+
+def swap(values, axis, bit):
+    size = lax.axis_size(axis)
+    return lax.ppermute(values, axis, [(i, i ^ bit) for i in range(size)])
+
+
+def cut_dim(shape):
+    return 1 if (shape[1] // 2) % 128 == 0 else 0
+
+
+def is_upper(axis, bit):
+    return (lax.axis_index(axis) & bit) != 0
+
+
+def halve(values, dim, axis, bit):
+    half = values.shape[dim] // 2
+    upper = is_upper(axis, bit).astype(jnp.int32)
+    mine = lax.dynamic_slice_in_dim(values, upper * half, half, dim)
+    other = lax.dynamic_slice_in_dim(values, (1 - upper) * half, half, dim)
+    return mine, other
+
+
+def join(mine, other, dim, axis, bit):
+    upper = is_upper(axis, bit)
+    return jnp.where(
+        upper,
+        jnp.concatenate([other, mine], axis=dim),
+        jnp.concatenate([mine, other], axis=dim),
+    )
+
+
+def cut_plan(shape):
+    plan = []
+    for bit in axis_bits("rep"):
+        dim = cut_dim(shape)
+        plan.append((bit, dim))
+        shape = tuple(n // 2 if i == dim else n for i, n in enumerate(shape))
+    return plan
+
+
+def spread_over_rep(piece, plan):
+    for bit, dim in reversed(plan):
+        piece = join(piece, swap(piece, "rep", bit), dim, "rep", bit)
+    return piece
+
+
+def gather_shard(shard):
+    plan = cut_plan(shard.shape)
+    piece = shard
+    for bit, dim in plan:
+        piece, _ = halve(piece, dim, "rep", bit)
+    count = lax.axis_size("fsdp")
+    if count == 2:
+        other = spread_over_rep(swap(piece, "fsdp", 1), plan)
+        return join(shard, other, 0, "fsdp", 1)
+    pieces = lax.all_gather(piece, "fsdp", axis=0)
+    return jnp.concatenate([spread_over_rep(pieces[i], plan) for i in range(count)], axis=0)
+
+
+def reduce_shard(whole):
+    count = lax.axis_size("fsdp")
+    rows = whole.shape[0] // count
+    plan = cut_plan((rows, whole.shape[1]))
+    held = whole.reshape(count, rows, whole.shape[1])
+    held = held.astype(jnp.bfloat16)
+
+    def step(held, dim, axis, bit):
+        mine, other = halve(held, dim, axis, bit)
+        return mine + swap(other, axis, bit)
+
+    for bit, dim in plan[:1]:
+        held = step(held, dim + 1, "rep", bit)
+    for bit in reversed(axis_bits("fsdp")):
+        held = step(held, 0, "fsdp", bit)
+    held = held[0]
+    for bit, dim in plan[1:]:
+        held = step(held, dim, "rep", bit)
+    return spread_over_rep(held, plan)
 
 
 def body(
@@ -71,18 +160,19 @@
     groups = QH // KVH
     softmax_scale = HD ** (-0.5)
     block_count = length // KEYBLK
-    gathered = (
-        lax.all_gather(q_weight, "fsdp", axis=0, tiled=True),
-        lax.all_gather(k_weight, "fsdp", axis=0, tiled=True),
-        lax.all_gather(v_weight, "fsdp", axis=0, tiled=True),
-        lax.all_gather(o_weight, "fsdp", axis=0, tiled=True),
-        lax.all_gather(gate_weight, "fsdp", axis=0, tiled=True),
-        lax.all_gather(up_weight, "fsdp", axis=0, tiled=True),
-        lax.all_gather(down_weight, "fsdp", axis=0, tiled=True),
-        lax.all_gather(attn_gain, "fsdp", axis=0, tiled=True),
-        lax.all_gather(ffn_gain, "fsdp", axis=0, tiled=True),
-    )
-    full_q, full_k, full_v, full_o, full_gate, full_up, full_down, gain_attn, gain_ffn = gathered
+    kv_width = KVH * HD
+    q_width = QH * HD
+    heads_shard = jnp.concatenate([q_weight, k_weight, v_weight, o_weight], axis=1)
+    heads_whole = gather_shard(heads_shard)
+    full_q = heads_whole[:, :q_width]
+    full_k = heads_whole[:, q_width : q_width + kv_width]
+    full_v = heads_whole[:, q_width + kv_width : q_width + 2 * kv_width]
+    full_o = heads_whole[:, q_width + 2 * kv_width :]
+    full_gate = gather_shard(gate_weight)
+    full_up = gather_shard(up_weight)
+    full_down = gather_shard(down_weight)
+    gains = lax.all_gather(jnp.stack([attn_gain, ffn_gain]), "fsdp", axis=1, tiled=True)
+    gain_attn, gain_ffn = gains[0], gains[1]
     positions = my_index * rows_here + jnp.arange(rows_here, dtype=jnp.int32)
     last_position = my_index * rows_here + rows_here - 1
     cosine_table, sine_table = rotary_tables(positions)
@@ -100,11 +190,11 @@
     )
     keys_low = keys_low.reshape(rows_here, KVH * HD)
     values_low = v_pre.astype(jnp.bfloat16)
-    all_keys, all_values, all_segments = (
-        lax.all_gather(keys_low, "fsdp", axis=0, tiled=True),
-        lax.all_gather(values_low, "fsdp", axis=0, tiled=True),
-        lax.all_gather(segments, "fsdp", axis=0, tiled=True),
-    )
+    both = lax.all_gather(
+        jnp.concatenate([keys_low, values_low], axis=1), "fsdp", axis=0, tiled=True
+    )
+    all_keys, all_values = both[:, :kv_width], both[:, kv_width:]
+    all_segments = lax.all_gather(segments, "fsdp", axis=0, tiled=True)
 
     def block_scores(block_index, key_source, segment_source):
         key_start = block_index * KEYBLK
@@ -185,20 +275,9 @@
     silu_gate = gate_pre * sigmoid_gate
     hidden_low = (silu_gate * up_pre).astype(jnp.bfloat16)
     result = middle + jnp.dot(hidden_low, full_down, preferred_element_type=jnp.float32)
-    back_set = (
-        lax.all_gather(q_weight, "fsdp", axis=0, tiled=True),
-        lax.all_gather(k_weight, "fsdp", axis=0, tiled=True),
-        lax.all_gather(v_weight, "fsdp", axis=0, tiled=True),
-        lax.all_gather(o_weight, "fsdp", axis=0, tiled=True),
-        lax.all_gather(gate_weight, "fsdp", axis=0, tiled=True),
-        lax.all_gather(up_weight, "fsdp", axis=0, tiled=True),
-        lax.all_gather(down_weight, "fsdp", axis=0, tiled=True),
-        lax.all_gather(attn_gain, "fsdp", axis=0, tiled=True),
-        lax.all_gather(ffn_gain, "fsdp", axis=0, tiled=True),
-    )
-    back_q, back_k, back_v, back_o, back_gate, back_up, back_down, back_gain_attn, back_gain_ffn = (
-        back_set
-    )
+    back_q, back_k, back_v, back_o = full_q, full_k, full_v, full_o
+    back_gate, back_up, back_down = full_gate, full_up, full_down
+    back_gain_attn, back_gain_ffn = gain_attn, gain_ffn
     key_source, value_source, segment_source = (all_keys, all_values, all_segments)
     cot_low = out_grad.astype(jnp.bfloat16)
     grad_down = jnp.einsum("tf,td->fd", hidden_low, cot_low, preferred_element_type=jnp.float32)
@@ -269,14 +348,10 @@
     )
     key_terms = key_terms.reshape(length, KVH * HD)
     value_terms = value_terms.reshape(length, KVH * HD)
-    d_keys_sum, d_values_sum = (
-        lax.psum_scatter(
-            key_terms.astype(jnp.bfloat16), "fsdp", scatter_dimension=0, tiled=True
-        ).astype(jnp.float32),
-        lax.psum_scatter(
-            value_terms.astype(jnp.bfloat16), "fsdp", scatter_dimension=0, tiled=True
-        ).astype(jnp.float32),
-    )
+    both_terms = jnp.concatenate([key_terms, value_terms], axis=1).astype(jnp.bfloat16)
+    both_sum = lax.psum_scatter(both_terms, "fsdp", scatter_dimension=0, tiled=True)
+    d_keys_sum = both_sum[:, :kv_width].astype(jnp.float32)
+    d_values_sum = both_sum[:, kv_width:].astype(jnp.float32)
     dq_low = (
         rotate_back(d_queries.reshape(rows_here, QH, HD), cosine_table, sine_table)
         .astype(jnp.bfloat16)
@@ -302,45 +377,24 @@
         activations, scale_one, back_gain_attn.astype(jnp.float32), d_normed_one
     )
     grad_activations = d_middle + d_norm_attn
-    shares = (
-        lax.psum_scatter(
-            grad_q.astype(jnp.bfloat16), "fsdp", scatter_dimension=0, tiled=True
-        ).astype(jnp.float32),
-        lax.psum_scatter(
-            grad_k.astype(jnp.bfloat16), "fsdp", scatter_dimension=0, tiled=True
-        ).astype(jnp.float32),
-        lax.psum_scatter(
-            grad_v.astype(jnp.bfloat16), "fsdp", scatter_dimension=0, tiled=True
-        ).astype(jnp.float32),
-        lax.psum_scatter(
-            grad_o.astype(jnp.bfloat16), "fsdp", scatter_dimension=0, tiled=True
-        ).astype(jnp.float32),
-        lax.psum_scatter(
-            grad_gate.astype(jnp.bfloat16), "fsdp", scatter_dimension=0, tiled=True
-        ).astype(jnp.float32),
-        lax.psum_scatter(
-            grad_up.astype(jnp.bfloat16), "fsdp", scatter_dimension=0, tiled=True
-        ).astype(jnp.float32),
-        lax.psum_scatter(
-            grad_down.astype(jnp.bfloat16), "fsdp", scatter_dimension=0, tiled=True
-        ).astype(jnp.float32),
-        lax.psum_scatter(
-            grad_attn_term.astype(jnp.bfloat16), "fsdp", scatter_dimension=0, tiled=True
-        ).astype(jnp.float32),
-        lax.psum_scatter(
-            grad_ffn_term.astype(jnp.bfloat16), "fsdp", scatter_dimension=0, tiled=True
-        ).astype(jnp.float32),
-    )
+    down_total = reduce_shard(grad_down).astype(jnp.float32)
+    gate_total = reduce_shard(grad_gate).astype(jnp.float32)
+    up_total = reduce_shard(grad_up).astype(jnp.float32)
+    heads_grad = jnp.concatenate([grad_q, grad_k, grad_v, grad_o], axis=1)
+    heads_total = reduce_shard(heads_grad).astype(jnp.float32)
+    gain_terms = jnp.stack([grad_attn_term, grad_ffn_term]).astype(jnp.bfloat16)
+    gain_share = lax.psum_scatter(gain_terms, "fsdp", scatter_dimension=1, tiled=True)
+    gain_total = lax.psum(gain_share, "rep").astype(jnp.float32)
     totals = (
-        lax.psum(shares[0].astype(jnp.bfloat16), "rep").astype(jnp.float32),
-        lax.psum(shares[1].astype(jnp.bfloat16), "rep").astype(jnp.float32),
-        lax.psum(shares[2].astype(jnp.bfloat16), "rep").astype(jnp.float32),
-        lax.psum(shares[3].astype(jnp.bfloat16), "rep").astype(jnp.float32),
-        lax.psum(shares[4].astype(jnp.bfloat16), "rep").astype(jnp.float32),
-        lax.psum(shares[5].astype(jnp.bfloat16), "rep").astype(jnp.float32),
-        lax.psum(shares[6].astype(jnp.bfloat16), "rep").astype(jnp.float32),
-        lax.psum(shares[7].astype(jnp.bfloat16), "rep").astype(jnp.float32),
-        lax.psum(shares[8].astype(jnp.bfloat16), "rep").astype(jnp.float32),
+        heads_total[:, :q_width],
+        heads_total[:, q_width : q_width + kv_width],
+        heads_total[:, q_width + kv_width : q_width + 2 * kv_width],
+        heads_total[:, q_width + 2 * kv_width :],
+        gate_total,
+        up_total,
+        down_total,
+        gain_total[0],
+        gain_total[1],
     )
     return (
         result,

time: 953 us -> 684 us (0.72)
  waiting for transfers between devices: 611 us -> 156 us
  starting transfers between devices: 0.86 us -> 111 us
  local copies, waits for them, and re-layouts: 40 us -> 117 us
  blocking collectives: 112 us -> 44.2 us
  other arithmetic: 39.7 us -> 104 us
    reduce_scatter x7 -> x1, waiting for transfers between devices: 316 us -> 0.01 us  [body(): lax.psum_scatter(both_terms, 'fsdp', scatter_dimension=0, tiled=True)]
    ppermute x0 -> x56, waiting for transfers between devices: none -> 156 us  [swap(): return lax.ppermute(values, axis, [(i, i ^ bit) for i in range(size)])]
    all_gather x5 -> x1, waiting for transfers between devices: 148 us -> 0.01 us  [body(): lax.all_gather(jnp.concatenate([keys_low, values_low], axis=1), 'fsdp', a...]
    psum x1 -> x0, waiting for transfers between devices: 141 us -> none  [body(): lax.psum(shares[0].astype(jnp.bfloat16), 'rep').astype(jnp.float32)]
    ppermute x0 -> x56, starting transfers between devices: none -> 111 us  [swap(): return lax.ppermute(values, axis, [(i, i ^ bit) for i in range(size)])]
    all_gather x5 -> x2, blocking collectives: 66.8 us -> 9.18 us  [the longest x1 4.85 us: body(): lax.all_gather(jnp.stack([attn_gain, ffn_gain]), 'fsdp', axis=1, tiled=True)]
    select_n x0 -> x29, other arithmetic: none -> 38.2 us  [join(): jnp.where(upper, jnp.concatenate([other, mine], axis=dim), jnp.concatenat...]
    dynamic_slice x0 -> x25, local copies, waits for them, and re-layouts: none -> 25 us  [the longest x21 19.7 us: halve(): other = lax.dynamic_slice_in_dim(values, (1 - upper) * half, half, dim)]
  transfers between devices with their start and end apart: 15 -> 59, of which waited for: 12 -> 24; matrix products, arithmetic and copies ran while one was open for 12% -> 32% of each run, Pallas kernels for 0% -> 0%
where the time goes in v1:
time: 684 us; the launch traced here: 675 us
  waiting for transfers between devices  156 us (23%)
  matrix products  124 us (18%)
  local copies, waits for them, and re-layouts  117 us (17%)
  starting transfers between devices  111 us (16%)
  other arithmetic  104 us (15%)
  blocking collectives  44.2 us (6%)
  between operations  15.6 us (2%)
    ppermute x56, waiting for transfers between devices, swap(): return lax.ppermute(values, axis, [(i, i ^ bit) for i in range(size)])  156 us
    ppermute x56, starting transfers between devices, swap(): return lax.ppermute(values, axis, [(i, i ^ bit) for i in range(size)])  111 us
    select_n x29, other arithmetic, join(): jnp.where(upper, jnp.concatenate([other, mine], axis=dim), jnp.concatenat...  38.2 us
    unnamed x151, local copies, waits for them, and re-layouts  36.6 us
    psum x1, blocking collectives, body(): gain_total = lax.psum(gain_share, 'rep').astype(jnp.float32)  35 us
    dynamic_slice x21, local copies, waits for them, and re-layouts, halve(): other = lax.dynamic_slice_in_dim(values, (1 - upper) * half, half, dim)  19.7 us
    add x20, other arithmetic, step(): return mine + swap(other, axis, bit)  18.7 us
    dot_general x2, matrix products, block_scores(): jnp.einsum('tkgd,skd->kgts', queries, key_block, preferred_element_type=j...  14.6 us
  transfers between devices with their start and end apart: 59, of which 24 were waited for; matrix products, arithmetic and copies ran while one was open for 32% of the time, Pallas kernels for 0%

profile of v1, /device:TPU:0, one launch (start us, length us, event | category | flops | bytes accessed | tf_op | source)
XLA Modules:
  0.0 675.0 jit_solution(10576080341836037424)
XLA Ops:
  89.4 10.5 %collective-permute-done.13 = bf16[480,640]{1,0:T(8,128)(2,1)S(1)} collective-permute-done((bf16[480,640]{1,0:T(8,128)(2,1)S(1)}, bf16[480,640]{1,0:T(8,128)(2,1)S(1)}, u32[]{:S(2)}, u32[]{:S(2)}) %collective-permute-start.13) | collective-permute-done | bytes 614432 | tf_op jit(solution)/shard_map/ppermute | solution.py:66
  101.2 9.7 %collective-permute-done.18 = bf16[320,960]{1,0:T(8,128)(2,1)S(1)} collective-permute-done((bf16[320,960]{1,0:T(8,128)(2,1)S(1)}, bf16[320,960]{1,0:T(8,128)(2,1)S(1)}, u32[]{:S(2)}, u32[]{:S(2)}) %collective-permute-start.18) | collective-permute-done | bytes 614432 | tf_op jit(solution)/shard_map/ppermute | solution.py:66
  139.5 9.1 %fusion.51 = f32[2560,512]{0,1:T(8,128)} fusion(bf16[1280,960]{1,0:T(8,128)(2,1)S(1)} %copy-done.30, bf16[1280,960]{1,0:T(8,128)(2,1)S(1)} %maximum_select_fusion.4, pred[]{:T(512)S(6)} %ne.10, f32[512,960]{0,1:T(8,128)S(1)} %copy-done.36), kind=kOutput, calls=%fused_computation.131 | convolution fusion | flops 2539192320 | bytes 12124161 | tf_op jit(solution)/shard_map/td,fd->tf/dot_general | solution.py:284
  150.0 16.7 %while.51 = (s32[]{:T(128)}, f32[5,3,512]{2,1,0:T(4,128)S(1)}, f32[5,3,512]{2,1,0:T(4,128)S(1)}, s32[]{:T(128)}, s32[512]{0:T(512)S(1)}, /*index=5*/s32[1024]{0:...) while((s32[]{:T(128)}, f32[5,3,512]{2,1,0:T(4,128)S(1)}, ...), condition=%wide.region_6.7_spmd.clone, body=%wide.region_1.6_spmd.clone.sunk | while | flops 535576576 | bytes 34629952 | solution.py:242
  150.1 16.6 %conditional.9 = ((f32[5,3,512]{2,1,0:T(4,128)S(1)}, f32[5,3,512]{2,1,0:T(4,128)S(1)})) conditional(s32[]{:T(128)} %convert_element_type.257, (f32[5,3,512]{2,1,0:T(4,128)S(1)}, f32[5,3,512]{2,1,0:T(4,128)S(1)}) %tuple.147, (s32[512]{0:T(512)S(1)}, s32[]{:T(128)}, s32[1024]{0:T(1024)S(1)}, s32[]{:T(128)}, bf16[1024,320]{0,1:T(8,128)(2,1)S(1)}, ...), branch_computations={%region_2.2_spmd, %region_3.5_spmd} | conditional | flops 535576576 | bytes 34627672 | solution.py:233
  157.4 9.2 %select_reduce_fusion = f32[5,3,512]{2,1,0:T(4,128)S(1)} fusion(f32[5,512,512,3]{2,1,3,0:T(8,128)} %get-tuple-element.767, f32[5,3,512]{2,1,0:T(4,128)S(1)} %max.2, pred[512,512]{0,1:T(8,128)(4,1)S(1)} %compare_and_fusion), kind=kLoop, calls=%fused_computation.4 | loop fusion | flops 19653120 | bytes 16052224 | tf_op jit(solution)/shard_map/while/body/eval_jaxpr/cond/branch_1_fun/reduce_sum | solution.py:230
  168.3 7.9 %while.52 = (s32[]{:T(128)}, f32[512,5,3,64]{0,3,2,1:T(8,128)}, s32[]{:T(128)}, bf16[1024,320]{0,1:T(8,128)(2,1)S(1)}, s32[512]{0:T(512)S(1)}, /*index=5*/s32[10...) while((s32[]{:T(128)}, f32[512,5,3,64]{0,3,2,1:T(8,128)}, ...), condition=%wide.region_10.11_spmd.clone, body=%wide.region_7.10_spmd.clone.sunk | while | flops 1023640576 | bytes 7457069 | solution.py:265
  168.5 7.7 %conditional.10 = (f32[512,5,3,64]{0,3,2,1:T(8,128)}) conditional(s32[]{:T(128)} %convert_element_type.258, f32[512,5,3,64]{0,3,2,1:T(8,128)} %get-tuple-element.1090, (s32[]{:T(128)}, bf16[1024,320]{0,1:T(8,128)(2,1)S(1)}, s32[512]{0:T(512)S(1)}, s32[1024]{0:T(1024)S(1)}, s32[]{:T(128)}, /*index=5*/bf16[1024,320]{0,1:T(8,128)(2,1)S(1)}, ...), branch_computations={%region_8.8_spmd, %region_9.9_spmd} | conditional | flops 1023640576 | bytes 7454790 | solution.py:258
  190.4 9.9 %fusion.26 = (bf16[512,2560]{1,0:T(8,128)(2,1)}, bf16[512,2560]{1,0:T(8,128)(2,1)}, bf16[512,2560]{1,0:T(8,128)(2,1)}) fusion(f32[2560,512]{0,1:T(8,128)} %fusion.51, f32[512,2560]{1,0:T(8,128)} %fusion.54, bf16[512,960]{0,1:T(8,128)(2,1)S(1)} %multiply_convert_fusion.1, bf16[480,2560]{1,0:T(8,128)(2,1)S(1)} %copy-done.51, ...), kind=kOutput, calls=%fused_computation.53 | convolution fusion | flops 2558361600 | bytes 24248320 | tf_op jit(solution)/shard_map/dot_general | solution.py:273
  223.0 39.2 %while.53 = (s32[]{:T(128)}, f32[512,5,3,64]{0,3,2,1:T(8,128)S(1)}, bf16[2,512,320]{1,2,0:T(8,128)(2,1)}, bf16[2,512,320]{1,2,0:T(8,128)(2,1)}, s32[2]{0:T(128)S...) while((s32[]{:T(128)}, f32[512,5,3,64]{0,3,2,1:T(8,128)S(1)}, ...), condition=%wide.region_16.17_spmd.clone, body=%wide.region_13.16_spmd.clone.sunk | while | flops 2558002176 | bytes 83802496 | solution.py:346
  224.5 31.9 %conditional.11 = (f32[512,5,3,64]{0,3,2,1:T(8,128)S(1)}, bf16[1,512,320]{1,2,0:T(8,128)(2,1)}, bf16[1,512,320]{1,2,0:T(8,128)(2,1)S(1)}) conditional(s32[]{:T(128)} %convert_element_type.259, f32[512,5,3,64]{0,3,2,1:T(8,128)S(1)} %get-tuple-element.1131, (s32[]{:T(128)}, bf16[1024,320]{0,1:T(8,128)(2,1)}, s32[512]{0:T(512)S(1)}, ...), branch_computations={%region_14.14_spmd, %region_15.15_spmd} | conditional | flops 2558002176 | bytes 82489432 | solution.py:343
  226.6 7.7 %fusion.85 = f32[5,512,512,3]{2,1,3,0:T(8,128)} fusion(bf16[512,5,64,1]{0,2,3,1:T(8,128)(2,1)S(1)} %bitcast.211, bf16[512,5,3,64]{0,3,2,1:T(8,128)(2,1)S(1)} %get-tuple-element.481), kind=kOutput, calls=%fused_computation.239 | convolution fusion | flops 503316480 | bytes 17039360 | tf_op jit(solution)/shard_map/while/body/eval_jaxpr/cond/branch_1_fun/tkgd,skd->kgts/dot_general | solution.py:206
  234.4 8.8 %fusion.18 = bf16[5,512,64,1]{1,2,3,0:T(8,128)(2,1)S(1)} fusion(bf16[512,5,3,64]{0,3,2,1:T(8,128)(2,1)} %get-tuple-element.484, f32[5,512,512,3]{2,1,3,0:T(8,128)} %fusion.85, f32[5,3,512]{2,1,0:T(4,128)S(1)} %get-tuple-element.482, pred[512,512]{0,1:T(8,128)(4,1)S(1)} %compare_and_fusion.2), kind=kOutput, calls=%fused_computation.31 | convolution fusion | flops 519045120 | bytes 17332224 | tf_op jit(solution)/shard_map/while/body/eval_jaxpr/cond/branch_1_fun/kgts,tkgd->skd/dot_general | solution.py:313
  243.1 8.6 %fusion.14 = bf16[5,3,512,512]{2,3,1,0:T(8,128)(2,1)S(1)} fusion(f32[5,512,512,3]{2,1,3,0:T(8,128)} %fusion.85, bf16[512,5,64,1]{0,2,3,1:T(8,128)(2,1)S(1)} %bitcast.221, bf16[512,5,3,64]{0,3,2,1:T(8,128)(2,1)} %get-tuple-element.484, f32[5,3,512]{2,1,0:T(4,128)S(1)} %get-tuple-element.485, f32[5,3,512]{2,1,0:T(4,128)S(1)} %get-tuple-element.482, ...), kind=kOutput, calls=%fused_computation.26 | convolution fusion | flops 526909440 | bytes 25227264 | tf_op jit(solution)/shard_map/while/body/eval_jaxpr/cond/branch_1_fun/tkgd,skd->kgts/dot_general | solution.py:319
  273.0 10.9 %convert_element_type.210 = bf16[2,1280,960]{1,0,2:T(2,128)(2,1)} reshape(bf16[2560,960]{0,1:T(8,128)(2,1)} %convolution_convert_fusion) | data formatting | bytes 9830400 | tf_op jit(solution)/shard_map/convert_element_type | solution.py:127
  325.6 56.2 %collective-permute-start.30 = (bf16[1,480,1280]{2,1,0:T(8,128)(2,1)}, bf16[1,480,1280]{2,1,0:T(8,128)(2,1)}, u32[]{:S(2)}, u32[]{:S(2)}) collective-permute-start(bf16[1,480,1280]{2,1,0:T(8,128)(2,1)} %constant_dynamic-slice_fusion.16), channel_id=1, source_target_pairs={{0,1},{1,0},{2,3},{3,2},{4,5},{5,4},{6,7},{7,6},{8,9},{9,8},{10,11... | collective-permute-start | bytes 3686408 | tf_op jit(solution)/shard_map/ppermute | solution.py:66
  410.5 8.7 %concatenate.314 = bf16[960,2560]{1,0:T(8,128)(2,1)} concatenate(bf16[960,960]{1,0:T(8,128)(2,1)} %convolution_convert_fusion.4, bf16[960,320]{1,0:T(8,128)(2,1)S(1)} %copy.121, bf16[960,320]{1,0:T(8,128)(2,1)S(1)} %copy.122, bf16[960,960]{1,0:T(8,128)(2,1)} %convolution_convert_fusion.3), dimensions={1} | concatenate | bytes 9830400 | tf_op jit(solution)/shard_map/concatenate | solution.py:383
  427.5 8.7 %collective-permute-done.39 = bf16[1,480,1280]{2,1,0:T(8,128)(2,1)} collective-permute-done((bf16[1,480,1280]{2,1,0:T(8,128)(2,1)}, bf16[1,480,1280]{2,1,0:T(8,128)(2,1)}, u32[]{:S(2)}, u32[]{:S(2)}) %collective-permute-start.39) | collective-permute-done | bytes 1228832 | tf_op jit(solution)/shard_map/ppermute | solution.py:66
  440.4 21.7 %collective-permute-done.48 = bf16[1,640,960]{1,2,0:T(8,128)(2,1)} collective-permute-done((bf16[1,640,960]{1,2,0:T(8,128)(2,1)}, bf16[1,640,960]{1,2,0:T(8,128)(2,1)}, u32[]{:S(2)}, u32[]{:S(2)}) %collective-permute-start.48) | collective-permute-done | bytes 1228832 | tf_op jit(solution)/shard_map/ppermute | solution.py:66
  487.5 9.3 %collective-permute-done.50 = bf16[160,960]{1,0:T(8,128)(2,1)S(1)} collective-permute-done((bf16[160,960]{1,0:T(8,128)(2,1)S(1)}, bf16[160,960]{1,0:T(8,128)(2,1)S(1)}, u32[]{:S(2)}, u32[]{:S(2)}) %collective-permute-start.50) | collective-permute-done | bytes 307232 | tf_op jit(solution)/shard_map/ppermute | solution.py:66
  507.0 7.4 %collective-permute-done.51 = bf16[80,960]{1,0:T(8,128)(2,1)S(1)} collective-permute-done((bf16[80,960]{1,0:T(8,128)(2,1)S(1)}, bf16[80,960]{1,0:T(8,128)(2,1)S(1)}, u32[]{:S(2)}, u32[]{:S(2)}) %collective-permute-start.51) | collective-permute-done | bytes 153632 | tf_op jit(solution)/shard_map/ppermute | solution.py:66
  534.6 19.6 %collective-permute-done.53 = bf16[160,960]{1,0:T(8,128)(2,1)S(1)} collective-permute-done((bf16[160,960]{1,0:T(8,128)(2,1)S(1)}, bf16[160,960]{1,0:T(8,128)(2,1)S(1)}, u32[]{:S(2)}, u32[]{:S(2)}) %collective-permute-start.53) | collective-permute-done | bytes 307232 | tf_op jit(solution)/shard_map/ppermute | solution.py:66
  576.0 9.4 %collective-permute-done.36 = bf16[480,640]{1,0:T(8,128)(2,1)} collective-permute-done((bf16[480,640]{1,0:T(8,128)(2,1)}, bf16[480,640]{1,0:T(8,128)(2,1)}, u32[]{:S(2)}, u32[]{:S(2)}) %collective-permute-start.36) | collective-permute-done | bytes 614432 | tf_op jit(solution)/shard_map/ppermute | solution.py:66
  596.2 35.0 %psum.7 = bf16[2,480]{1,0:T(2,128)(2,1)S(1)} all-reduce(bf16[2,480]{1,0:T(2,128)(2,1)S(1)} %copy.154), channel_id=1, replica_groups=mesh['rep'=16,'fsdp'=2] {'rep'}, use_global_device_ids=true, to_apply=%region_22.23 | all-reduce | flops 960 | bytes 3840 | tf_op jit(solution)/shard_map/psum | solution.py:387
  (463 shorter events, 397.2 us)
Async XLA Ops:
  7.2 141.5 %all-gather.4.cloned.1.call-start = ((), (), s32[]{:S(2)}) async-start(), calls=%async_computation.2 | async-start | bytes 1966080 | tf_op jit(solution)/shard_map/all_gather | solution.py:193
  9.0 44.7 %collective-permute-start.10 = (bf16[120,640]{1,0:T(8,128)(2,1)}, bf16[120,640]{1,0:T(8,128)(2,1)S(1)}, u32[]{:S(2)}, u32[]{:S(2)}) collective-permute-start(bf16[120,640]{1,0:T(8,128)(2,1)} %dynamic_slice.210), channel_id=1, source_target_pairs={{0,1},{1,0},{2,3},{3,2},{4,5},{5,4},{6,7},{7,6},{8,9},{9,8},{10,11... | collective-permute-start | bytes 460808 | tf_op jit(solution)/shard_map/ppermute | solution.py:66
  13.7 31.0 %collective-permute-start.5 = (bf16[120,640]{1,0:T(8,128)(2,1)}, bf16[120,640]{1,0:T(8,128)(2,1)S(1)}, u32[]{:S(2)}, u32[]{:S(2)}) collective-permute-start(bf16[120,640]{1,0:T(8,128)(2,1)} %dynamic_slice.209), channel_id=1, source_target_pairs={{0,1},{1,0},{2,3},{3,2},{4,5},{5,4},{6,7},{7,6},{8,9},{9,8},{10,11... | collective-permute-start | bytes 460808 | tf_op jit(solution)/shard_map/ppermute | solution.py:66
  71.1 41.9 %collective-permute-start.4 = (bf16[480,1280]{1,0:T(8,128)(2,1)S(1)}, bf16[480,1280]{1,0:T(8,128)(2,1)}, u32[]{:S(2)}, u32[]{:S(2)}) collective-permute-start(bf16[480,1280]{1,0:T(8,128)(2,1)S(1)} %maximum_select_fusion.14), channel_id=1, source_target_pairs={{0,2},{2,0},{4,6},{6,4},{8,10},{10,8},{12,14},{14,12},{16,18},{18,... | collective-permute-start | bytes 3686408 | tf_op jit(solution)/shard_map/ppermute | solution.py:66
  89.4 35.4 %collective-permute-start.9 = (bf16[480,1280]{1,0:T(8,128)(2,1)}, bf16[480,1280]{1,0:T(8,128)(2,1)}, u32[]{:S(2)}, u32[]{:S(2)}) collective-permute-start(bf16[480,1280]{1,0:T(8,128)(2,1)} %maximum_select_fusion.15), channel_id=1, source_target_pairs={{0,2},{2,0},{4,6},{6,4},{8,10},{10,8},{12,14},{14,12},{16,18},{18,... | collective-permute-start | bytes 3686408 | tf_op jit(solution)/shard_map/ppermute | solution.py:66
  120.5 277.9 %reduce-scatter.5.cloned.1.call-start = ((), (), s32[]{:S(2)}) async-start(), calls=%async_computation.3 | async-start | bytes 1966080 | tf_op jit(solution)/shard_map/reduce_scatter | solution.py:352
  265.7 329.5 %reduce-scatter.7.cloned.1.call-start = ((), (), s32[]{:S(2)}) async-start(), calls=%async_computation.4 | async-start | bytes 368640
  287.5 34.5 %collective-permute-start.29 = (bf16[2,480,1280]{2,1,0:T(8,128)(2,1)}, bf16[2,480,1280]{2,1,0:T(8,128)(2,1)}, u32[]{:S(2)}, u32[]{:S(2)}) collective-permute-start(bf16[2,480,1280]{2,1,0:T(8,128)(2,1)} %constant_dynamic-slice_fusion.17), channel_id=1, source_target_pairs={{0,2},{2,0},{4,6},{6,4},{8,10},{10,8},{12,14},{14,12},{16,18},{18,... | collective-permute-start | bytes 7372808 | tf_op jit(solution)/shard_map/ppermute | solution.py:66
  298.9 82.8 %collective-permute-start.38 = (bf16[2,480,1280]{2,1,0:T(8,128)(2,1)}, bf16[2,480,1280]{2,1,0:T(8,128)(2,1)}, u32[]{:S(2)}, u32[]{:S(2)}) collective-permute-start(bf16[2,480,1280]{2,1,0:T(8,128)(2,1)} %constant_dynamic-slice_fusion.13), channel_id=1, source_target_pairs={{0,2},{2,0},{4,6},{6,4},{8,10},{10,8},{12,14},{14,12},{16,18},{18,... | collective-permute-start | bytes 7372808 | tf_op jit(solution)/shard_map/ppermute | solution.py:66
  299.2 86.8 %collective-permute-start.47 = (bf16[2,640,960]{1,2,0:T(8,128)(2,1)}, bf16[2,640,960]{1,2,0:T(8,128)(2,1)}, u32[]{:S(2)}, u32[]{:S(2)}) collective-permute-start(bf16[2,640,960]{1,2,0:T(8,128)(2,1)} %copy.156), channel_id=1, source_target_pairs={{0,2},{2,0},{4,6},{6,4},{8,10},{10,8},{12,14},{14,12},{16,18},{18,... | collective-permute-start | bytes 7372808 | tf_op jit(solution)/shard_map/ppermute | solution.py:66
  325.6 97.6 %collective-permute-start.30 = (bf16[1,480,1280]{2,1,0:T(8,128)(2,1)}, bf16[1,480,1280]{2,1,0:T(8,128)(2,1)}, u32[]{:S(2)}, u32[]{:S(2)}) collective-permute-start(bf16[1,480,1280]{2,1,0:T(8,128)(2,1)} %constant_dynamic-slice_fusion.16), channel_id=1, source_target_pairs={{0,1},{1,0},{2,3},{3,2},{4,5},{5,4},{6,7},{7,6},{8,9},{9,8},{10,11... | collective-permute-start | bytes 3686408 | tf_op jit(solution)/shard_map/ppermute | solution.py:66
  386.0 50.2 %collective-permute-start.39 = (bf16[1,480,1280]{2,1,0:T(8,128)(2,1)}, bf16[1,480,1280]{2,1,0:T(8,128)(2,1)}, u32[]{:S(2)}, u32[]{:S(2)}) collective-permute-start(bf16[1,480,1280]{2,1,0:T(8,128)(2,1)} %constant_dynamic-slice_fusion.12), channel_id=1, source_target_pairs={{0,1},{1,0},{2,3},{3,2},{4,5},{5,4},{6,7},{7,6},{8,9},{9,8},{10,11... | collective-permute-start | bytes 3686408 | tf_op jit(solution)/shard_map/ppermute | solution.py:66
  396.4 65.8 %collective-permute-start.48 = (bf16[1,640,960]{1,2,0:T(8,128)(2,1)}, bf16[1,640,960]{1,2,0:T(8,128)(2,1)}, u32[]{:S(2)}, u32[]{:S(2)}) collective-permute-start(bf16[1,640,960]{1,2,0:T(8,128)(2,1)} %copy.126), channel_id=1, source_target_pairs={{0,1},{1,0},{2,3},{3,2},{4,5},{5,4},{6,7},{7,6},{8,9},{9,8},{10,11... | collective-permute-start | bytes 3686408 | tf_op jit(solution)/shard_map/ppermute | solution.py:66
  422.6 49.6 %collective-permute-start.20 = (bf16[2,480,1280]{2,1,0:T(8,128)(2,1)}, bf16[2,480,1280]{2,1,0:T(8,128)(2,1)}, u32[]{:S(2)}, u32[]{:S(2)}) collective-permute-start(bf16[2,480,1280]{2,1,0:T(8,128)(2,1)} %constant_dynamic-slice_fusion.21), channel_id=1, source_target_pairs={{0,2},{2,0},{4,6},{6,4},{8,10},{10,8},{12,14},{14,12},{16,18},{18,... | collective-permute-start | bytes 7372808 | tf_op jit(solution)/shard_map/ppermute | solution.py:66
  425.8 41.7 %collective-permute-start.31 = (bf16[480,640]{1,0:T(8,128)(2,1)}, bf16[480,640]{1,0:T(8,128)(2,1)}, u32[]{:S(2)}, u32[]{:S(2)}) collective-permute-start(bf16[480,640]{1,0:T(8,128)(2,1)} %dynamic-slice_bitcast_fusion.2), channel_id=1, source_target_pairs={{0,4},{2,6},{4,0},{6,2},{8,12},{10,14},{12,8},{14,10},{16,20},{18,... | collective-permute-start | bytes 1843208 | tf_op jit(solution)/shard_map/ppermute | solution.py:66
  438.6 31.9 %collective-permute-start.40 = (bf16[480,640]{1,0:T(8,128)(2,1)}, bf16[480,640]{1,0:T(8,128)(2,1)}, u32[]{:S(2)}, u32[]{:S(2)}) collective-permute-start(bf16[480,640]{1,0:T(8,128)(2,1)} %dynamic-slice_bitcast_fusion.1), channel_id=1, source_target_pairs={{0,4},{2,6},{4,0},{6,2},{8,12},{10,14},{12,8},{14,10},{16,20},{18,... | collective-permute-start | bytes 1843208 | tf_op jit(solution)/shard_map/ppermute | solution.py:66
  475.3 27.8 %collective-permute-start.21 = (bf16[1,480,1280]{2,1,0:T(8,128)(2,1)S(1)}, bf16[1,480,1280]{2,1,0:T(8,128)(2,1)S(1)}, u32[]{:S(2)}, u32[]{:S(2)}) collective-permute-start(bf16[1,480,1280]{2,1,0:T(8,128)(2,1)S(1)} %constant_dynamic-slice_fusion.20), channel_id=1, source_target_pairs={{0,1},{1,0},{2,3},{3,2},{4,5},{5,4},{6,7},{7,6},{8,9},{9,8},{10,11... | collective-permute-start | bytes 3686408 | tf_op jit(solution)/shard_map/ppermute | solution.py:66
  519.1 36.6 %collective-permute-start.35 = (bf16[240,640]{1,0:T(8,128)(2,1)S(1)}, bf16[240,640]{1,0:T(8,128)(2,1)S(1)}, u32[]{:S(2)}, u32[]{:S(2)}) collective-permute-start(bf16[240,640]{1,0:T(8,128)(2,1)S(1)} %maximum_select_fusion.40), channel_id=1, source_target_pairs={{0,8},{2,10},{4,12},{6,14},{8,0},{10,2},{12,4},{14,6},{16,24},{18,... | collective-permute-start | bytes 921608 | tf_op jit(solution)/shard_map/ppermute | solution.py:66
  524.6 36.7 %collective-permute-start.44 = (bf16[240,640]{1,0:T(8,128)(2,1)S(1)}, bf16[240,640]{1,0:T(8,128)(2,1)S(1)}, u32[]{:S(2)}, u32[]{:S(2)}) collective-permute-start(bf16[240,640]{1,0:T(8,128)(2,1)S(1)} %maximum_select_fusion.41), channel_id=1, source_target_pairs={{0,8},{2,10},{4,12},{6,14},{8,0},{10,2},{12,4},{14,6},{16,24},{18,... | collective-permute-start | bytes 921608 | tf_op jit(solution)/shard_map/ppermute | solution.py:66
  556.8 28.6 %collective-permute-start.36 = (bf16[480,640]{1,0:T(8,128)(2,1)}, bf16[480,640]{1,0:T(8,128)(2,1)}, u32[]{:S(2)}, u32[]{:S(2)}) collective-permute-start(bf16[480,640]{1,0:T(8,128)(2,1)} %maximum_select_fusion.32), channel_id=1, source_target_pairs={{0,4},{2,6},{4,0},{6,2},{8,12},{10,14},{12,8},{14,10},{16,20},{18,... | collective-permute-start | bytes 1843208 | tf_op jit(solution)/shard_map/ppermute | solution.py:66
  562.4 68.8 %collective-permute-start.45 = (bf16[480,640]{1,0:T(8,128)(2,1)}, bf16[480,640]{1,0:T(8,128)(2,1)}, u32[]{:S(2)}, u32[]{:S(2)}) collective-permute-start(bf16[480,640]{1,0:T(8,128)(2,1)} %maximum_select_fusion.33), channel_id=1, source_target_pairs={{0,4},{2,6},{4,0},{6,2},{8,12},{10,14},{12,8},{14,10},{16,20},{18,... | collective-permute-start | bytes 1843208 | tf_op jit(solution)/shard_map/ppermute | solution.py:66
  576.0 58.9 %collective-permute-start.55 = (bf16[640,960]{0,1:T(8,128)(2,1)}, bf16[640,960]{0,1:T(8,128)(2,1)}, u32[]{:S(2)}, u32[]{:S(2)}) collective-permute-start(bf16[640,960]{0,1:T(8,128)(2,1)} %copy.128), channel_id=1, source_target_pairs={{0,2},{2,0},{4,6},{6,4},{8,10},{10,8},{12,14},{14,12},{16,18},{18,... | collective-permute-start | bytes 3686408 | tf_op jit(solution)/shard_map/ppermute | solution.py:66
  588.4 60.4 %collective-permute-start.37 = (bf16[480,1280]{1,0:T(8,128)(2,1)}, bf16[480,1280]{1,0:T(8,128)(2,1)}, u32[]{:S(2)}, u32[]{:S(2)}) collective-permute-start(bf16[480,1280]{1,0:T(8,128)(2,1)} %maximum_select_fusion.18), channel_id=1, source_target_pairs={{0,2},{2,0},{4,6},{6,4},{8,10},{10,8},{12,14},{14,12},{16,18},{18,... | collective-permute-start | bytes 3686408 | tf_op jit(solution)/shard_map/ppermute | solution.py:66
  590.6 45.8 %collective-permute-start.27 = (bf16[480,640]{1,0:T(8,128)(2,1)}, bf16[480,640]{1,0:T(8,128)(2,1)}, u32[]{:S(2)}, u32[]{:S(2)}) collective-permute-start(bf16[480,640]{1,0:T(8,128)(2,1)} %maximum_select_fusion.31), channel_id=1, source_target_pairs={{0,4},{2,6},{4,0},{6,2},{8,12},{10,14},{12,8},{14,10},{16,20},{18,... | collective-permute-start | bytes 1843208 | tf_op jit(solution)/shard_map/ppermute | solution.py:66
  (105 other events, 1245.5 us)
Sparse Core Ops, SparseCore 0:
  120.6 23.5 all-gather.3
  265.8 77.8 reduce-scatter.4
  561.5 10.8 reduce-scatter.6
